TPU v7x, 32 devices: a whole 2x2x4 slice. The times are simulated.
32 devices in a mesh: pole: 4 (over y, x), dom: 8 (over z, core).
Axes of the slice: x: 2, y: 2, z: 4, core: 2. Of those that a mesh axis runs over, the one named last changes fastest.
Arguments:
- y_interior: float32 [8, 512, 256], P('dom', 'pole'), may hold values from -6 to 6
- y_separator: float32 [8, 64, 256], P('dom'), may hold values from -6 to 6
- green: float32 [2, 4, 8, 512, 512], P(None, 'pole', 'dom'), as said below
- pole_data: float32 [4, 4], P(None, 'pole'), as said below
- coupling: float32 [8, 2, 64, 128], P('dom')
- sep_block: float32 [8, 64, 64], P('dom'), as said below
- iface_rows: int32 [8, 2, 128], P('dom'), may hold values from 0 to 511, as said below
Outputs:
- filtered: float32 [8, 512, 256], P('dom', 'pole')
- filtered_sep: float32 [8, 64, 256], P('dom', 'pole')
Inputs may be any that keep to these rules, and one draw needn't show every extreme that they name: green[:, p, d] holds the real and imaginary parts of the inverse of z[p] I - H[d], where H[d] is a real symmetric matrix of order 512 and z[p] is the pole of pole_data. `pole_data`: every pole lies in the upper half plane with imaginary part 0.3 or more. `sep_block`: each block is symmetric. iface_rows[d, 0] and iface_rows[d, 1] each list 128 distinct rows of domain d, and no row is in both.
All inputs are finite; a program needn't handle non-finite values.
Results may differ from a plain program's by a relative error of at most 0.00095.
Values sent between devices are 32-bit elements; how exact they have to be, the bound alone decides.
A program may use at most 64 MiB of HBM per device.

v0:
```python
import functools
import jax
import jax.numpy as jnp
from jax import lax
from jax.experimental import pallas as pl
from jax.experimental.pallas import tpu as pltpu
from jax.sharding import PartitionSpec as P

MESH = pl.DeviceIdType.MESH
f32 = jnp.float32


def dot(a, b, ca=1, cb=0):
    return lax.dot_general(
        a, b, (((ca,), (cb,)), ((), ())), precision=lax.Precision.HIGHEST, preferred_element_type=f32
    )


def lanes_below(shape, limit):
    return lax.broadcasted_iota(jnp.int32, shape, 1) < limit


def swap(value, half):
    return pltpu.roll(value, half, 1)


def small_inverse(dr, di):
    n = len(dr)
    row = lax.broadcasted_iota(jnp.int32, dr[0].shape, 0)
    for k in range(n):
        pr, pi = dr[k][k : k + 1], di[k][k : k + 1]
        scale = 1.0 / (pr * pr + pi * pi)
        qr, qi = pr * scale, -pi * scale
        here = row == k
        cr, ci = dr[k], di[k]
        new_r, new_i = [], []
        for m in range(n):
            if m == k:
                new_r.append(jnp.where(here, qr, ci * qi - cr * qr))
                new_i.append(jnp.where(here, qi, -(cr * qi + ci * qr)))
            else:
                tr, ti = dr[m][k : k + 1], di[m][k : k + 1]
                rr, ri = tr * qr - ti * qi, tr * qi + ti * qr
                new_r.append(jnp.where(here, rr, dr[m] - cr * rr + ci * ri))
                new_i.append(jnp.where(here, ri, di[m] - cr * ri - ci * rr))
        dr, di = new_r, new_i
    return dr, di


def inverse(packed):
    n = packed.shape[0]
    step = 8
    lane = lax.broadcasted_iota(jnp.int32, packed.shape, 1)
    within = lax.rem(lane, n)
    swept = within < step
    sign = jnp.where(lane[:step] < n, -1.0, 1.0)
    unit = (lane[:step] == lax.broadcasted_iota(jnp.int32, (step, 2 * n), 0)).astype(f32)

    def body(_, a):
        shape = a.shape
        col_r = [jnp.broadcast_to(a[:, m : m + 1], shape) for m in range(step)]
        col_i = [jnp.broadcast_to(a[:, n + m : n + m + 1], shape) for m in range(step)]
        inv_r, inv_i = small_inverse([c[:step] for c in col_r], [c[:step] for c in col_i])
        top = jnp.where(swept[:step], unit, a[:step])
        turned = swap(top, n) * sign
        r = jnp.zeros_like(top)
        ri = jnp.zeros_like(top)
        for m in range(step):
            tm, um = top[m : m + 1], turned[m : m + 1]
            r = r + inv_r[m] * tm + inv_i[m] * um
            ri = ri + inv_r[m] * um - inv_i[m] * tm
        rest = jnp.where(swept[step:], 0.0, a[step:])
        for m in range(step):
            rest = rest - col_r[m][step:] * r[m : m + 1] - col_i[m][step:] * ri[m : m + 1]
        full = jnp.concatenate([rest, r], axis=0)
        return jnp.where(within < n - step, pltpu.roll(full, 2 * n - step, 1), pltpu.roll(full, n - step, 1))

    return lax.fori_loop(0, n // step, body, packed)


def embed(re, im):
    return jnp.concatenate(
        [jnp.concatenate([re, im], axis=1), jnp.concatenate([-im, re], axis=1)], axis=0
    )


def embed_packed(packed):
    n = packed.shape[1] // 2
    turned = swap(packed, n) * jnp.where(lanes_below(packed.shape, n), -1.0, 1.0)
    return jnp.concatenate([packed, turned], axis=0)


def kernel(
    poles, doms, y_ref, ysep_ref, green_ref, pole_ref, coup_ref, sep_ref, rows_ref,
    out_ref, outsep_ref,
    ybuf, part, part_sep, got, got_sep, sbuf, sgot, tbufs, tgots, xsends, xgots, first, maps,
    y_s, y_r, s_s, s_r, t_s, t_r, x_s, x_r, o_s, o_r, p_s, p_r,
):
    levels = doms.bit_length() - 1
    pole = lax.axis_index("pole")
    dom = lax.axis_index("dom")
    bits = [lax.rem(lax.div(dom, 1 << l), 2) for l in range(levels)]
    mates = [dom + (1 - 2 * bits[l]) * (1 << l) for l in range(levels)]
    peers = [lax.rem(pole + o, poles) for o in range(1, poles)]

    def send(src, dst, send_sem, recv_sem, place):
        copy = pltpu.make_async_remote_copy(
            src_ref=src, dst_ref=dst, send_sem=send_sem, recv_sem=recv_sem,
            device_id=place, device_id_type=MESH,
        )
        copy.start()
        return copy

    barrier = pltpu.get_barrier_semaphore()
    for peer in peers:
        pl.semaphore_signal(barrier, inc=1, device_id=(peer, dom), device_id_type=MESH)
    for mate in mates:
        pl.semaphore_signal(barrier, inc=1, device_id=(pole, mate), device_id_type=MESH)
    pl.semaphore_wait(barrier, len(peers) + len(mates))

    sent = []
    y_copies = [
        send(y_ref, ybuf.at[pole], y_s.at[o], y_r.at[o], (peer, dom)) for o, peer in enumerate(peers)
    ]
    ybuf[pole] = y_ref[...]

    s = sep_ref.shape[0]
    ni = green_ref.shape[1]
    m = y_ref.shape[1]
    zr, zi, wr, wi = pole_ref[0], pole_ref[1], pole_ref[2], pole_ref[3]
    spot = lax.broadcasted_iota(jnp.int32, (rows_ref.shape[1], ni), 1)
    pick_u = (rows_ref[0] == spot).astype(f32)
    pick_w = (rows_ref[1] == spot).astype(f32)
    has_left = (dom > 0).astype(f32)
    c = jnp.concatenate([dot(coup_ref[1] * has_left, pick_w), dot(coup_ref[0], pick_u)], axis=0)
    n_r = dot(c, green_ref[0])
    n_i = dot(c, green_ref[1])
    k_r = dot(n_r, c, 1, 1)
    k_i = dot(n_i, c, 1, 1)
    eye = (
        lax.broadcasted_iota(jnp.int32, (s, s), 0) == lax.broadcasted_iota(jnp.int32, (s, s), 1)
    ).astype(f32)
    gap = jnp.zeros((s, s), f32)
    corner_r = zr * eye - sep_ref[...]
    corner_i = zi * eye

    def place_corner(block):
        low = jnp.concatenate([gap, block], axis=1)
        return jnp.concatenate([jnp.zeros_like(low), low], axis=0)

    own = jnp.concatenate([place_corner(corner_r) - k_r, place_corner(corner_i) - k_i], axis=1)
    sbuf[0] = own
    s_copies = [send(sbuf.at[0], sgot.at[0], s_s.at[0], s_r.at[0], (pole, mates[0]))]

    maps[:, : 2 * s] = jnp.transpose(wr * n_r - wi * n_i)
    maps[:, 2 * s :] = jnp.transpose(-(wr * n_i + wi * n_r))

    for copy in y_copies:
        copy.wait_recv()
    y_all = ybuf[...].reshape(ni, m)
    right_r = jnp.transpose(dot(n_r, y_all))
    right_i = jnp.transpose(dot(n_i, y_all))
    sep_t = jnp.transpose(jnp.concatenate([jnp.zeros((s, m), f32), ysep_ref[...]], axis=0))
    t = jnp.concatenate([right_r + sep_t, right_i], axis=1)

    low = lanes_below((s, 2 * s), s)
    kept = []
    t_copies = []
    for l in range(levels):
        width = t.shape[0] // 2
        tbufs[l][0] = t[:width]
        tbufs[l][1] = t[width:]
        t_copies.append(
            send(tbufs[l].at[1 - bits[l]], tgots[l], t_s.at[l], t_r.at[l], (pole, mates[l]))
        )
        if l == 0:
            weighted = wr * green_ref[0] - wi * green_ref[1]
            first[...] = dot(weighted, y_all)
        is_low = bits[l] == 0
        s_copies[l].wait_recv()
        mine, other = sbuf[l], sgot[l]
        left = jnp.where(is_low, mine, other)
        right = jnp.where(is_low, other, mine)
        lr, li = left[:, : 2 * s], left[:, 2 * s :]
        rr, ri = right[:, : 2 * s], right[:, 2 * s :]
        p_r_ = swap(lr[s:], s) + rr[:s]
        p_i_ = swap(li[s:], s) + ri[:s]
        pivot = jnp.where(low, p_r_, swap(p_i_, s))
        y_re = jnp.where(low, lr[s:], rr[:s])
        y_im = jnp.where(low, li[s:], ri[:s])
        turned = jnp.transpose(jnp.concatenate([y_re, y_im], axis=0))
        pinv = inverse(pivot)
        z = dot(pinv, embed(y_re, y_im))
        z_re, z_im = z[:, : 2 * s], z[:, 2 * s :]
        z_emb = embed(z_re, z_im)
        base = jnp.concatenate(
            [
                jnp.concatenate([jnp.where(low, lr[:s], 0.0), jnp.where(low, li[:s], 0.0)], axis=1),
                jnp.concatenate([jnp.where(low, 0.0, rr[s:]), jnp.where(low, 0.0, ri[s:])], axis=1),
            ],
            axis=0,
        )
        merged = base - dot(turned, z_emb)
        if l + 1 < levels:
            sbuf[l + 1] = merged
            s_copies.append(
                send(sbuf.at[l + 1], sgot.at[l + 1], s_s.at[l + 1], s_r.at[l + 1], (pole, mates[l + 1]))
            )
        t_copies[l].wait_recv()
        t_mine, t_other = tbufs[l][bits[l]], tgots[l][...]
        t_left = jnp.where(is_low, t_mine, t_other)
        t_right = jnp.where(is_low, t_other, t_mine)
        below = lanes_below((width, 2 * s), s)
        sum_r = swap(t_left[:, : 2 * s], s) + t_right[:, : 2 * s]
        sum_i = swap(t_left[:, 2 * s :], s) + t_right[:, 2 * s :]
        middle = jnp.where(below, sum_r, swap(sum_i, s))
        ends = jnp.concatenate(
            [
                jnp.where(below, t_left[:, : 2 * s], t_right[:, : 2 * s]),
                jnp.where(below, t_left[:, 2 * s :], t_right[:, 2 * s :]),
            ],
            axis=1,
        )
        t = ends - dot(middle, z_emb)
        back = jnp.concatenate(
            [jnp.concatenate([z_re, -z_im], axis=1), jnp.concatenate([z_im, z_re], axis=1)], axis=0
        )
        kept.append((dot(middle, embed_packed(pinv)), back, below))

    width = t.shape[0]
    below = lanes_below((width, 2 * s), s)
    pivot = jnp.where(low, swap(merged[s:, : 2 * s], s), merged[s:, 2 * s :])
    rhs = jnp.where(below, swap(t[:, : 2 * s], s), t[:, 2 * s :])
    x_end = dot(rhs, embed_packed(inverse(pivot)))
    x = jnp.concatenate(
        [jnp.where(below, 0.0, swap(x_end, s)), jnp.where(below, 0.0, x_end)], axis=1
    )
    x_copies = []
    for l in reversed(range(levels)):
        part_m, back, below = kept[l]
        xm = part_m - dot(x, back, 1, 1)
        xr, xi = x[:, : 2 * s], x[:, 2 * s :]
        xm_t = swap(xm, s)
        x_left = jnp.concatenate([jnp.where(below, xr, xm_t), jnp.where(below, xi, xm)], axis=1)
        x_right = jnp.concatenate([jnp.where(below, xm, xr), jnp.where(below, xm_t, xi)], axis=1)
        is_low = bits[l] == 0
        xsends[l][...] = jnp.where(is_low, x_right, x_left)
        copy = send(xsends[l], xgots[l].at[bits[l]], x_s.at[l], x_r.at[l], (pole, mates[l]))
        xgots[l][bits[l]] = jnp.where(is_low, x_left, x_right)
        copy.wait_recv()
        x_copies.append(copy)
        x = xgots[l][...].reshape(-1, 4 * s)

    rows = ni // poles
    for q in range(poles):
        part[q] = first[q * rows : (q + 1) * rows] + dot(maps[q * rows : (q + 1) * rows], x, 1, 1)
    o_copies = [
        send(part.at[peer], got.at[o], o_s.at[o], o_r.at[o], (peer, dom)) for o, peer in enumerate(peers)
    ]
    weighted_sep = jnp.transpose(wr * x[:, : 2 * s] - wi * x[:, 2 * s :])[s:]
    rows_sep = s // poles
    for q in range(poles):
        part_sep[q] = weighted_sep[q * rows_sep : (q + 1) * rows_sep]
    p_copies = [
        send(part_sep.at[peer], got_sep.at[o], p_s.at[o], p_r.at[o], (peer, dom))
        for o, peer in enumerate(peers)
    ]
    total = part[pole]
    for o in range(len(peers)):
        o_copies[o].wait_recv()
        total = total + got[o]
    out_ref[...] = total
    total = part_sep[pole]
    for o in range(len(peers)):
        p_copies[o].wait_recv()
        total = total + got_sep[o]
    outsep_ref[...] = total
    for copy in y_copies + s_copies + t_copies + x_copies + o_copies + p_copies:
        copy.wait_send()


def shards(poles, doms, y_interior, y_separator, green, pole_data, coupling, sep_block, iface_rows):
    rows, m = y_interior.shape[1:]
    s = sep_block.shape[-1]
    ni = green.shape[-1]
    levels = doms.bit_length() - 1
    others = max(poles - 1, 1)
    vmem = pl.BlockSpec(memory_space=pltpu.VMEM)
    dma = pltpu.SemaphoreType.DMA
    buf = lambda *shape: pltpu.VMEM(shape, f32)
    widths = [m >> (l + 1) for l in range(levels)]
    out, out_sep = pl.pallas_call(
        functools.partial(kernel, poles, doms),
        out_shape=(
            jax.ShapeDtypeStruct((rows, m), f32),
            jax.ShapeDtypeStruct((s // poles, m), f32),
        ),
        in_specs=[vmem, vmem, vmem, pl.BlockSpec(memory_space=pltpu.SMEM), vmem, vmem, vmem],
        out_specs=(vmem, vmem),
        scratch_shapes=[
            buf(poles, rows, m),
            buf(poles, rows, m),
            buf(poles, s // poles, m),
            buf(others, rows, m),
            buf(others, s // poles, m),
            buf(levels, 2 * s, 4 * s),
            buf(levels, 2 * s, 4 * s),
            [buf(2, w, 4 * s) for w in widths],
            [buf(w, 4 * s) for w in widths],
            [buf(w, 4 * s) for w in widths],
            [buf(2, w, 4 * s) for w in widths],
            buf(ni, m),
            buf(ni, 4 * s),
            dma((others,)), dma((others,)),
            dma((levels,)), dma((levels,)),
            dma((levels,)), dma((levels,)),
            dma((levels,)), dma((levels,)),
            dma((others,)), dma((others,)),
            dma((others,)), dma((others,)),
        ],
        compiler_params=pltpu.CompilerParams(
            collective_id=0, has_side_effects=True, vmem_limit_bytes=40 * 1024 * 1024
        ),
    )(
        y_interior[0], y_separator[0], green[:, 0, 0], pole_data[:, 0], coupling[0], sep_block[0],
        iface_rows[0][:, :, None],
    )
    return out[None], out_sep[None]


def solution(mesh):
    return jax.shard_map(
        functools.partial(shards, mesh.shape["pole"], mesh.shape["dom"]),
        mesh=mesh,
        in_specs=(
            P("dom", "pole", None),
            P("dom", None, None),
            P(None, "pole", "dom", None, None),
            P(None, "pole"),
            P("dom", None, None, None),
            P("dom", None, None),
            P("dom", None, None),
        ),
        out_specs=(P("dom", "pole", None), P("dom", "pole", None)),
        check_vma=False,
    )
```

profile of v0, /device:TPU:0, one launch (start us, length us, event | category | flops | bytes accessed | tf_op | source)
XLA Modules:
  0.0 67.6 jit_solution(2535022159970758498)
XLA Ops:
  0.6 0.8 %copy.9.rows_ref = s32[2,128,1]{2,1,0:T(8,128)S(1)} copy(s32[2,128,1]{1,0,2:T(2,128)} %bitcast.17) | data formatting | bytes 2048 | tf_op jit(solution)/shard_map/broadcast_in_dim;squeeze | solution.py:326
  1.4 0.0 copy-start
  1.5 1.6 %copy-done = f32[2,1,1,512,512]{4,3,2,1,0:T(8,128)S(1)} copy-done((f32[2,1,1,512,512]{4,3,2,1,0:T(8,128)S(1)}, f32[2,1,1,512,512]{4,3,2,1,0:T(8,128)}, u32[]{:S(2)}) %copy-start) | copy-done | bytes 2097176
  3.0 0.0 copy-start.1
  3.0 0.9 %copy-done.1 = f32[1,128,256]{2,1,0:T(8,128)S(1)} copy-done((f32[1,128,256]{2,1,0:T(8,128)S(1)}, f32[1,128,256]{2,1,0:T(8,128)}, u32[]{:S(2)}) %copy-start.1) | copy-done | bytes 131096
  3.9 0.0 copy-start.2
  3.9 0.8 %copy-done.2 = f32[1,64,256]{2,1,0:T(8,128)S(1)} copy-done((f32[1,64,256]{2,1,0:T(8,128)S(1)}, f32[1,64,256]{2,1,0:T(8,128)}, u32[]{:S(2)}) %copy-start.2) | copy-done | bytes 65560
  4.8 0.0 copy-start.3
  4.8 0.8 %copy-done.3 = f32[1,2,64,128]{3,2,1,0:T(8,128)S(1)} copy-done((f32[1,2,64,128]{3,2,1,0:T(8,128)S(1)}, f32[1,2,64,128]{3,2,1,0:T(8,128)}, u32[]{:S(2)}) %copy-start.3) | copy-done | bytes 65560
  5.6 0.0 copy-start.4
  5.6 0.8 %copy-done.4 = f32[1,64,64]{2,1,0:T(8,128)S(1)} copy-done((f32[1,64,64]{2,1,0:T(8,128)S(1)}, f32[1,64,64]{2,1,0:T(8,128)}, u32[]{:S(2)}) %copy-start.4) | copy-done | bytes 16408
  6.4 0.0 copy-start.5
  6.4 0.7 copy-done.5
  7.0 59.3 %shard_map.86 = (f32[128,256]{1,0:T(8,128)S(1)}, f32[16,256]{1,0:T(8,128)S(1)}) custom-call(f32[128,256]{1,0:T(8,128)S(1)} %bitcast.10, f32[64,256]{1,0:T(8,128)S(1)} %bitcast.12, f32[2,512,512]{2,1,0:T(8,128)S(1)} %bitcast.9, f32[4]{0:T(128)S(1)} %bitcast.16, f32[2,64,128]{2,1,0:T(8,128)S(1)} %bitcast.13, f32[64,64]{1,0:T(8,128)S(1)} %bitcast.14, ...), custom_call_target="tpu_custom_call" | custom-call | tf_op jit(solution)/shard_map/pallas_call | solution.py:292
  66.3 0.7 copy.12
  67.0 0.6 copy.13
Async XLA Ops:
  1.4 1.6 %copy-start = (f32[2,1,1,512,512]{4,3,2,1,0:T(8,128)S(1)}, f32[2,1,1,512,512]{4,3,2,1,0:T(8,128)}, u32[]{:S(2)}) copy-start(f32[2,1,1,512,512]{4,3,2,1,0:T(8,128)} %param.9) | copy-start | bytes 6291460
  3.0 0.9 %copy-start.1 = (f32[1,128,256]{2,1,0:T(8,128)S(1)}, f32[1,128,256]{2,1,0:T(8,128)}, u32[]{:S(2)}) copy-start(f32[1,128,256]{2,1,0:T(8,128)} %param.7) | copy-start | bytes 393220
  3.9 0.8 %copy-start.2 = (f32[1,64,256]{2,1,0:T(8,128)S(1)}, f32[1,64,256]{2,1,0:T(8,128)}, u32[]{:S(2)}) copy-start(f32[1,64,256]{2,1,0:T(8,128)} %param.8) | copy-start | bytes 196612
  4.8 0.8 %copy-start.3 = (f32[1,2,64,128]{3,2,1,0:T(8,128)S(1)}, f32[1,2,64,128]{3,2,1,0:T(8,128)}, u32[]{:S(2)}) copy-start(f32[1,2,64,128]{3,2,1,0:T(8,128)} %param.11) | copy-start | bytes 196612
  5.6 0.8 %copy-start.4 = (f32[1,64,64]{2,1,0:T(8,128)S(1)}, f32[1,64,64]{2,1,0:T(8,128)}, u32[]{:S(2)}) copy-start(f32[1,64,64]{2,1,0:T(8,128)} %param.12) | copy-start | bytes 49156
  6.4 0.7 copy-start.5
where the time goes:
time: 67.9 us; the launch traced here: 67.6 us
  Pallas kernels  59.3 us (87%)
  local copies, waits for them, and re-layouts  7.65 us (11%)
    pallas_call x1, Pallas kernels, shards(): pl.pallas_call(functools.partial(kernel, poles, doms), out_shape=(jax.Sha...  59.3 us
    unnamed x14, local copies, waits for them, and re-layouts  6.85 us

commit v1 on v0

v1 whole, which is shorter than its diff:
```python
import functools
import jax
import jax.numpy as jnp
from jax import lax
from jax.experimental import pallas as pl
from jax.experimental.pallas import tpu as pltpu
from jax.sharding import PartitionSpec as P

MESH = pl.DeviceIdType.MESH
f32 = jnp.float32


def split(value):
    high = value.astype(jnp.bfloat16)
    return high, (value - high.astype(f32)).astype(jnp.bfloat16)


def dot(a, b, ca=1, cb=0):
    a_high, a_low = a if isinstance(a, tuple) else split(a)
    b_high, b_low = b if isinstance(b, tuple) else split(b)

    def one(u, v):
        return lax.dot_general(u, v, (((ca,), (cb,)), ((), ())), preferred_element_type=f32)

    return one(a_high, b_high) + (one(a_high, b_low) + one(a_low, b_high))


def lanes_below(shape, limit):
    return lax.broadcasted_iota(jnp.int32, shape, 1) < limit


def swap(value, half):
    return pltpu.roll(value, half, 1)


def small_inverse(dr, di):
    n = len(dr)
    row = lax.broadcasted_iota(jnp.int32, dr[0].shape, 0)
    for k in range(n):
        pr, pi = dr[k][k : k + 1], di[k][k : k + 1]
        scale = 1.0 / (pr * pr + pi * pi)
        qr, qi = pr * scale, -pi * scale
        here = row == k
        cr, ci = dr[k], di[k]
        new_r, new_i = [], []
        for m in range(n):
            if m == k:
                new_r.append(jnp.where(here, qr, ci * qi - cr * qr))
                new_i.append(jnp.where(here, qi, -(cr * qi + ci * qr)))
            else:
                tr, ti = dr[m][k : k + 1], di[m][k : k + 1]
                rr, ri = tr * qr - ti * qi, tr * qi + ti * qr
                new_r.append(jnp.where(here, rr, dr[m] - cr * rr + ci * ri))
                new_i.append(jnp.where(here, ri, di[m] - cr * ri - ci * rr))
        dr, di = new_r, new_i
    return dr, di


def inverse(packed):
    n = packed.shape[0]
    step, steps = 8, 4
    lane = lax.broadcasted_iota(jnp.int32, packed.shape, 1)
    within = lax.rem(lane, n)
    sign = jnp.where(lane[:step] < n, -1.0, 1.0)
    row = lax.broadcasted_iota(jnp.int32, (step, 2 * n), 0)

    def body(_, a):
        shape = a.shape
        for b in range(steps):
            at = b * step
            swept = (within >= at) & (within < at + step)
            unit = (lane[:step] == row + at).astype(f32)
            col_r = [jnp.broadcast_to(a[:, at + m : at + m + 1], shape) for m in range(step)]
            col_i = [jnp.broadcast_to(a[:, n + at + m : n + at + m + 1], shape) for m in range(step)]
            inv_r, inv_i = small_inverse(
                [c[at : at + step] for c in col_r], [c[at : at + step] for c in col_i]
            )
            top = jnp.where(swept[:step], unit, a[at : at + step])
            turned = swap(top, n) * sign
            r = jnp.zeros_like(top)
            ri = jnp.zeros_like(top)
            for m in range(step):
                tm, um = top[m : m + 1], turned[m : m + 1]
                r = r + inv_r[m] * tm + inv_i[m] * um
                ri = ri + inv_r[m] * um - inv_i[m] * tm
            rest = jnp.where(swept, 0.0, a)
            for m in range(step):
                rest = rest - col_r[m] * r[m : m + 1] - col_i[m] * ri[m : m + 1]
            pieces = [rest[:at], r, rest[at + step :]] if at else [r, rest[step:]]
            a = jnp.concatenate(pieces, axis=0)
        move = step * steps
        a = jnp.concatenate([a[move:], a[:move]], axis=0)
        return jnp.where(within < n - move, pltpu.roll(a, 2 * n - move, 1), pltpu.roll(a, n - move, 1))

    return lax.fori_loop(0, n // (step * steps), body, packed)


def embed(re, im):
    return jnp.concatenate(
        [jnp.concatenate([re, im], axis=1), jnp.concatenate([-im, re], axis=1)], axis=0
    )


def embed_packed(packed):
    n = packed.shape[1] // 2
    turned = swap(packed, n) * jnp.where(lanes_below(packed.shape, n), -1.0, 1.0)
    return jnp.concatenate([packed, turned], axis=0)


def kernel(
    poles, doms, y_hbm, ysep_hbm, green_hbm, pole_ref, coup_hbm, sep_hbm, rows_hbm,
    out_ref, outsep_ref,
    ysep_ref, green_ref, coup_ref, sep_ref, rows_ref,
    ybuf, part, part_sep, got, got_sep, sbuf, sgot, ebuf, egot, tbufs, tgots, xsends, xgots, first, maps,
    load, y_s, y_r, s_s, s_r, t_s, t_r, x_s, x_r, o_s, o_r, p_s, p_r,
):
    levels = doms.bit_length() - 1
    top = levels - 1
    pole = lax.axis_index("pole")
    dom = lax.axis_index("dom")
    bits = [lax.rem(lax.div(dom, 1 << l), 2) for l in range(levels)]
    mates = [dom + (1 - 2 * bits[l]) * (1 << l) for l in range(levels)]
    peers = [lax.rem(pole + o, poles) for o in range(1, poles)]

    def fetch(src, dst, number):
        copy = pltpu.make_async_copy(src, dst, load.at[number])
        copy.start()
        return copy

    def send(src, dst, send_sem, recv_sem, place):
        copy = pltpu.make_async_remote_copy(
            src_ref=src, dst_ref=dst, send_sem=send_sem, recv_sem=recv_sem,
            device_id=place, device_id_type=MESH,
        )
        copy.start()
        return copy

    loads = [
        fetch(rows_hbm, rows_ref, 0),
        fetch(coup_hbm, coup_ref, 1),
        fetch(green_hbm, green_ref, 2),
        fetch(sep_hbm, sep_ref, 3),
        fetch(y_hbm, ybuf.at[pole], 4),
        fetch(ysep_hbm, ysep_ref, 5),
    ]
    barrier = pltpu.get_barrier_semaphore()
    for peer in peers:
        pl.semaphore_signal(barrier, inc=1, device_id=(peer, dom), device_id_type=MESH)
    for mate in mates:
        pl.semaphore_signal(barrier, inc=1, device_id=(pole, mate), device_id_type=MESH)
    pl.semaphore_wait(barrier, len(peers) + len(mates))
    y_copies = [
        send(y_hbm, ybuf.at[pole], y_s.at[o], y_r.at[o], (peer, dom)) for o, peer in enumerate(peers)
    ]

    s = sep_ref.shape[0]
    ni = green_ref.shape[1]
    m = y_hbm.shape[1]
    zr, zi, wr, wi = pole_ref[0, 0], pole_ref[1, 0], pole_ref[2, 0], pole_ref[3, 0]
    for copy in loads[:2]:
        copy.wait()
    spot = lax.broadcasted_iota(jnp.int32, (ni, rows_ref.shape[1]), 0)
    pick_u = (spot == rows_ref[0:1]).astype(f32)
    pick_w = (spot == rows_ref[1:2]).astype(f32)
    has_left = (dom > 0).astype(f32)
    c = split(
        jnp.concatenate([dot(coup_ref[1] * has_left, pick_w, 1, 1), dot(coup_ref[0], pick_u, 1, 1)], axis=0)
    )
    for copy in loads[2:4]:
        copy.wait()
    n_r = dot(c, green_ref[0])
    n_i = dot(c, green_ref[1])
    n_rs, n_is = split(n_r), split(n_i)
    k_r = dot(n_rs, c, 1, 1)
    k_i = dot(n_is, c, 1, 1)
    eye = (
        lax.broadcasted_iota(jnp.int32, (s, s), 0) == lax.broadcasted_iota(jnp.int32, (s, s), 1)
    ).astype(f32)
    gap = jnp.zeros((s, s), f32)

    def place_corner(block):
        under = jnp.concatenate([gap, block], axis=1)
        return jnp.concatenate([jnp.zeros_like(under), under], axis=0)

    corner_r, corner_i = zr * eye - sep_ref[...], zi * eye
    merged = jnp.concatenate([place_corner(corner_r) - k_r, place_corner(corner_i) - k_i], axis=1)
    low = lanes_below((s, 2 * s), s)
    kept = []
    s_copies, t_copies, x_copies = [], [], []

    def send_matrix(l):
        sbuf[l] = merged
        s_copies.append(send(sbuf.at[l], sgot.at[l], s_s.at[l], s_r.at[l], (pole, mates[l])))

    def send_rights(l, t):
        width = t.shape[0] // 2
        tbufs[l][0] = t[:width]
        tbufs[l][1] = t[width:]
        t_copies.append(
            send(tbufs[l].at[1 - bits[l]], tgots[l], t_s.at[l], t_r.at[l], (pole, mates[l]))
        )

    if top:
        send_matrix(0)
    maps[:, : 2 * s] = jnp.transpose(wr * n_r - wi * n_i)
    maps[:, 2 * s :] = jnp.transpose(-(wr * n_i + wi * n_r))
    halves = 2
    wide = m // halves

    def start_rights():
        for copy in loads[4:]:
            copy.wait()
        for copy in y_copies:
            copy.wait_recv()
        y_all = split(ybuf[...].reshape(ni, m))
        right_r = jnp.transpose(dot(n_rs, y_all))
        right_i = jnp.transpose(dot(n_is, y_all))
        sep_t = jnp.transpose(jnp.concatenate([jnp.zeros((s, m), f32), ysep_ref[...]], axis=0))
        return jnp.concatenate([right_r + sep_t, right_i], axis=1), y_all

    def merge_rights(l, z_emb, pinv_emb, back):
        t_copies[l].wait_recv()
        width = tgots[l].shape[0]
        is_low = bits[l] == 0
        t_mine, t_other = tbufs[l][bits[l]], tgots[l][...]
        t_left = jnp.where(is_low, t_mine, t_other)
        t_right = jnp.where(is_low, t_other, t_mine)
        below = lanes_below((width, 2 * s), s)
        sum_r = swap(t_left[:, : 2 * s], s) + t_right[:, : 2 * s]
        sum_i = swap(t_left[:, 2 * s :], s) + t_right[:, 2 * s :]
        middle = split(jnp.where(below, sum_r, swap(sum_i, s)))
        ends = jnp.concatenate(
            [
                jnp.where(below, t_left[:, : 2 * s], t_right[:, : 2 * s]),
                jnp.where(below, t_left[:, 2 * s :], t_right[:, 2 * s :]),
            ],
            axis=1,
        )
        kept.append((dot(middle, pinv_emb), back, below))
        return ends - dot(middle, z_emb)

    y_all = None
    t = None
    for l in range(top):
        is_low = bits[l] == 0
        s_copies[l].wait_recv()
        mine, other = sbuf[l], sgot[l]
        left = jnp.where(is_low, mine, other)
        right = jnp.where(is_low, other, mine)
        lr, li = left[:, : 2 * s], left[:, 2 * s :]
        rr, ri = right[:, : 2 * s], right[:, 2 * s :]
        pivot = jnp.where(low, swap(lr[s:], s) + rr[:s], swap(swap(li[s:], s) + ri[:s], s))
        y_re = jnp.where(low, lr[s:], rr[:s])
        y_im = jnp.where(low, li[s:], ri[:s])
        turned = split(jnp.transpose(jnp.concatenate([y_re, y_im], axis=0)))
        y_emb = split(embed(y_re, y_im))
        base = jnp.concatenate(
            [
                jnp.concatenate([jnp.where(low, lr[:s], 0.0), jnp.where(low, li[:s], 0.0)], axis=1),
                jnp.concatenate([jnp.where(low, 0.0, rr[s:]), jnp.where(low, 0.0, ri[s:])], axis=1),
            ],
            axis=0,
        )
        pinv = inverse(pivot)
        z = dot(pinv, y_emb)
        z_re, z_im = z[:, : 2 * s], z[:, 2 * s :]
        z_emb = split(embed(z_re, z_im))
        merged = base - dot(turned, z_emb)
        back = split(
            jnp.concatenate(
                [jnp.concatenate([z_re, -z_im], axis=1), jnp.concatenate([z_im, z_re], axis=1)], axis=0
            )
        )
        if l + 1 < top:
            send_matrix(l + 1)
        if l == 0:
            t, y_all = start_rights()
            send_rights(0, t)
            if l + 1 < top:
                weighted = wr * green_ref[0] - wi * green_ref[1]
                first[...] = dot(weighted, y_all)
        if l + 1 < top:
            t = merge_rights(l, z_emb, embed_packed(pinv), back)
            send_rights(l + 1, t)
        last = (z_emb, pinv, back)
    if not top:
        t, y_all = start_rights()
    if top < 2:
        weighted = wr * green_ref[0] - wi * green_ref[1]
        first[...] = dot(weighted, y_all)

    upper = bits[top] == 1
    end_pivot = jnp.where(low, swap(merged[s:, : 2 * s], s), merged[s:, 2 * s :])
    end_row = jnp.where(low, merged[s:, : 2 * s], swap(merged[s:, 2 * s :], s))
    end_col = jnp.where(low, swap(merged[:s, : 2 * s], s), merged[:s, 2 * s :])
    near = jnp.where(low, merged[:s, : 2 * s], swap(merged[:s, 2 * s :], s))
    row_emb = split(embed_packed(end_row))
    end_inv = inverse(end_pivot)
    end_z = dot(end_inv, row_emb)
    end_emb = split(embed_packed(end_z))
    ebuf[...] = jnp.where(upper, near - dot(end_col, end_emb), end_pivot)
    s_copies.append(send(ebuf, egot, s_s.at[top], s_r.at[top], (pole, mates[top])))
    if top:
        z_emb, pinv, back = last
        t = merge_rights(top - 1, z_emb, embed_packed(pinv), back)
    width = t.shape[0]
    below = lanes_below((width, 2 * s), s)
    t_end = jnp.where(below, swap(t[:, : 2 * s], s), t[:, 2 * s :])
    t_near = jnp.where(below, t[:, : 2 * s], swap(t[:, 2 * s :], s))
    t_ends = split(t_end)
    send_rights(top, jnp.where(upper, t_near - dot(t_ends, end_emb), t_end))
    x_part = dot(t_ends, embed_packed(end_inv))
    end_back = split(jnp.concatenate([jnp.where(low, end_z, -end_z), swap(end_z, s)], axis=0))
    s_copies[top].wait_recv()
    middle_inv = split(embed_packed(inverse(ebuf[...] + egot[...])))
    t_copies[top].wait_recv()
    xsends[top][...] = dot(tbufs[top][bits[top]] + tgots[top][...], middle_inv)

    def trade(l):
        copy = send(xsends[l], xgots[l].at[bits[l]], x_s.at[l], x_r.at[l], (pole, mates[l]))
        x_copies.append(copy)
        return copy

    copy = trade(top)
    xgots[top][bits[top]] = xsends[top][...]
    copy.wait_recv()
    xm = xgots[top][...].reshape(width, 2 * s)
    xm_t = swap(xm, s)
    x_end = x_part - dot(xm, end_back, 1, 1)
    x_end_t = swap(x_end, s)
    zero = jnp.zeros_like(xm)
    x = jnp.where(
        upper,
        jnp.concatenate([jnp.where(below, xm, x_end_t), jnp.where(below, xm_t, x_end)], axis=1),
        jnp.concatenate([jnp.where(below, zero, xm_t), jnp.where(below, zero, xm)], axis=1),
    )
    for l in reversed(range(top)):
        part_m, back, below = kept[l]
        xm = part_m - dot(x, back, 1, 1)
        xr, xi = x[:, : 2 * s], x[:, 2 * s :]
        xm_t = swap(xm, s)
        x_left = jnp.concatenate([jnp.where(below, xr, xm_t), jnp.where(below, xi, xm)], axis=1)
        x_right = jnp.concatenate([jnp.where(below, xm, xr), jnp.where(below, xm_t, xi)], axis=1)
        is_low = bits[l] == 0
        xsends[l][...] = jnp.where(is_low, x_right, x_left)
        copy = trade(l)
        xgots[l][bits[l]] = jnp.where(is_low, x_left, x_right)
        if l:
            copy.wait_recv()
            x = xgots[l][...].reshape(-1, 4 * s)
    if not top:
        xgots[0 if top else 1][...] = x.reshape(2, wide, 4 * s)

    rows = ni // poles
    rows_sep = s // poles
    o_copies, p_copies = [], []
    for turn in range(halves):
        half = bits[0] if turn == 0 else 1 - bits[0]
        columns = pl.ds(pl.multiple_of(half * wide, wide), wide)
        if turn and top:
            copy.wait_recv()
        xh = xgots[0 if top else 1][half]
        xhs = split(xh)
        for o, peer in enumerate(peers + [pole]):
            at = pl.ds(pl.multiple_of(peer * rows, rows), rows)
            part[turn, peer] = first[at, columns] + dot(maps[at, :], xhs, 1, 1)
            if o < len(peers):
                o_copies.append(
                    send(
                        part.at[turn, peer], got.at[o, :, columns],
                        o_s.at[turn, o], o_r.at[turn, o], (peer, dom),
                    )
                )
        weighted_sep = jnp.transpose(wr * xh[:, : 2 * s] - wi * xh[:, 2 * s :])[s:]
        for q in range(poles):
            part_sep[q, :, columns] = weighted_sep[q * rows_sep : (q + 1) * rows_sep]
    for o, peer in enumerate(peers):
        p_copies.append(
            send(part_sep.at[peer], got_sep.at[o], p_s.at[o], p_r.at[o], (peer, dom))
        )
    for turn in range(halves):
        half = bits[0] if turn == 0 else 1 - bits[0]
        columns = pl.ds(pl.multiple_of(half * wide, wide), wide)
        out_ref[:, columns] = part[turn, pole]
    for copy in o_copies:
        copy.wait_recv()
    total = out_ref[...]
    for o in range(len(peers)):
        total = total + got[o]
    out_ref[...] = total
    total = part_sep[pole]
    for o in range(len(peers)):
        p_copies[o].wait_recv()
        total = total + got_sep[o]
    outsep_ref[...] = total
    for copy in y_copies + s_copies + t_copies + x_copies + o_copies + p_copies:
        copy.wait_send()


def shards(poles, doms, y_interior, y_separator, green, pole_data, coupling, sep_block, iface_rows):
    rows, m = y_interior.shape[1:]
    s = sep_block.shape[-1]
    ni = green.shape[-1]
    levels = doms.bit_length() - 1
    others = max(poles - 1, 1)
    b = iface_rows.shape[-1]
    vmem = pl.BlockSpec(memory_space=pltpu.VMEM)
    hbm = pl.BlockSpec(memory_space=pl.ANY)
    dma = pltpu.SemaphoreType.DMA
    buf = lambda *shape: pltpu.VMEM(shape, f32)
    widths = [m >> (l + 1) for l in range(levels)]
    cols = [4 * s] * (levels - 1) + [2 * s]
    sizes = list(zip(widths, cols))
    out, out_sep = pl.pallas_call(
        functools.partial(kernel, poles, doms),
        out_shape=(
            jax.ShapeDtypeStruct((rows, m), f32),
            jax.ShapeDtypeStruct((s // poles, m), f32),
        ),
        in_specs=[hbm, hbm, hbm, pl.BlockSpec(memory_space=pltpu.SMEM), hbm, hbm, hbm],
        out_specs=(vmem, vmem),
        scratch_shapes=[
            buf(s, m),
            buf(2, ni, ni),
            buf(2, s, b),
            buf(s, s),
            pltpu.VMEM((2, b), jnp.int32),
            buf(poles, rows, m),
            buf(2, poles, rows, m // 2),
            buf(poles, s // poles, m),
            buf(others, rows, m),
            buf(others, s // poles, m),
            buf(max(levels - 1, 1), 2 * s, 4 * s),
            buf(max(levels - 1, 1), 2 * s, 4 * s),
            buf(s, 2 * s),
            buf(s, 2 * s),
            [buf(2, w, c) for w, c in sizes],
            [buf(w, c) for w, c in sizes],
            [buf(w, c) for w, c in sizes],
            [buf(2, w, c) for w, c in sizes] + [buf(2, m // 2, 4 * s)],
            buf(ni, m),
            buf(ni, 4 * s),
            dma((6,)),
            dma((others,)), dma((others,)),
            dma((levels,)), dma((levels,)),
            dma((levels,)), dma((levels,)),
            dma((levels,)), dma((levels,)),
            dma((2, others)), dma((2, others)),
            dma((others,)), dma((others,)),
        ],
        compiler_params=pltpu.CompilerParams(
            collective_id=0, has_side_effects=True, vmem_limit_bytes=56 * 1024 * 1024
        ),
    )(
        y_interior[0], y_separator[0], green[:, 0, 0], pole_data, coupling[0], sep_block[0],
        iface_rows[0],
    )
    return out[None], out_sep[None]


def solution(mesh):
    return jax.shard_map(
        functools.partial(shards, mesh.shape["pole"], mesh.shape["dom"]),
        mesh=mesh,
        in_specs=(
            P("dom", "pole", None),
            P("dom", None, None),
            P(None, "pole", "dom", None, None),
            P(None, "pole"),
            P("dom", None, None, None),
            P("dom", None, None),
            P("dom", None, None),
        ),
        out_specs=(P("dom", "pole", None), P("dom", "pole", None)),
        check_vma=False,
    )
```

time: 67.9 us -> 52.1 us (0.77)
  Pallas kernels: 59.3 us -> 46.9 us
  local copies, waits for them, and re-layouts: 7.65 us -> 4.2 us
    pallas_call x1, Pallas kernels: 59.3 us -> 46.9 us  [shards(): pl.pallas_call(functools.partial(kernel, poles, doms), out_shape=(jax.Sha...]
    unnamed x14 -> x3, local copies, waits for them, and re-layouts: 6.85 us -> 4.2 us
    another operation x1 -> x0, local copies, waits for them, and re-layouts: 0.81 us -> none  [shards(): iface_rows[0][:, :, None]]
where the time goes in v1:
time: 52.1 us; the launch traced here: 51.8 us
  Pallas kernels  46.9 us (90%)
  local copies, waits for them, and re-layouts  4.2 us (8%)
  between operations  0.64 us (1%)
    pallas_call x1, Pallas kernels, shards(): pl.pallas_call(functools.partial(kernel, poles, doms), out_shape=(jax.Sha...  46.9 us
    unnamed x3, local copies, waits for them, and re-layouts  4.2 us

profile of v1, /device:TPU:0, one launch (start us, length us, event | category | flops | bytes accessed | tf_op | source)
XLA Modules:
  0.0 51.8 jit_solution(13599808472047020394)
XLA Ops:
  0.6 1.3 %copy.9.pole_ref = f32[4,1]{1,0:T(4,128)} copy(f32[4,1]{0,1:T(1,128)} %param.10) | data formatting | bytes 32 | tf_op args[3]
  1.9 46.9 %shard_map.86 = (f32[128,256]{1,0:T(8,128)}, f32[16,256]{1,0:T(8,128)}) custom-call(f32[128,256]{1,0:T(8,128)} %bitcast.9, f32[64,256]{1,0:T(8,128)} %bitcast.11, f32[2,512,512]{2,1,0:T(8,128)} %bitcast.8, f32[4,1]{1,0:T(4,128)} %copy.9.pole_ref, f32[2,64,128]{2,1,0:T(8,128)} %bitcast.12, f32[64,64]{1,0:T(8,128)} %bitcast.13, s32[2,128]{1,0:T(2,128)} %bitcast.15), custom_call_target="tpu_custom_call" | custom-call | tf_op jit(solution)/shard_map/pallas_call | solution.py:414
  48.9 1.6 %copy.12 = f32[1,128,256]{2,1,0:T(8,128)} copy(f32[1,128,256]{2,1,0:T(8,128)} %bitcast.10) | data formatting | bytes 262144
  50.5 1.3 %copy.13 = f32[1,16,256]{2,1,0:T(8,128)} copy(f32[1,16,256]{2,1,0:T(8,128)} %bitcast.14) | data formatting | bytes 32768

commit v2 on v1

--- a/solution.py
+++ b/solution.py
@@ -33,27 +33,29 @@
     return pltpu.roll(value, half, 1)
 
 
-def small_inverse(dr, di):
+def sweep_rows(dr, di, top, turned):
     n = len(dr)
-    row = lax.broadcasted_iota(jnp.int32, dr[0].shape, 0)
+    row = lax.broadcasted_iota(jnp.int32, top.shape, 0)
     for k in range(n):
         pr, pi = dr[k][k : k + 1], di[k][k : k + 1]
         scale = 1.0 / (pr * pr + pi * pi)
         qr, qi = pr * scale, -pi * scale
         here = row == k
         cr, ci = dr[k], di[k]
-        new_r, new_i = [], []
-        for m in range(n):
-            if m == k:
-                new_r.append(jnp.where(here, qr, ci * qi - cr * qr))
-                new_i.append(jnp.where(here, qi, -(cr * qi + ci * qr)))
-            else:
-                tr, ti = dr[m][k : k + 1], di[m][k : k + 1]
-                rr, ri = tr * qr - ti * qi, tr * qi + ti * qr
-                new_r.append(jnp.where(here, rr, dr[m] - cr * rr + ci * ri))
-                new_i.append(jnp.where(here, ri, di[m] - cr * ri - ci * rr))
-        dr, di = new_r, new_i
-    return dr, di
+
+        def reduced(re, im):
+            tr, ti = re[k : k + 1], im[k : k + 1]
+            rr, ri = tr * qr - ti * qi, tr * qi + ti * qr
+            return (
+                jnp.where(here, rr, re - cr * rr + ci * ri),
+                jnp.where(here, ri, im - cr * ri - ci * rr),
+            )
+
+        later = [reduced(dr[m], di[m]) for m in range(k + 1, n)]
+        dr = dr[: k + 1] + [pair[0] for pair in later]
+        di = di[: k + 1] + [pair[1] for pair in later]
+        top, turned = reduced(top, turned)
+    return top, turned
 
 
 def inverse(packed):
@@ -61,7 +63,7 @@
     step, steps = 8, 4
     lane = lax.broadcasted_iota(jnp.int32, packed.shape, 1)
     within = lax.rem(lane, n)
-    sign = jnp.where(lane[:step] < n, -1.0, 1.0)
+    sign = jnp.where(lane[:step] < n, 1.0, -1.0)
     row = lax.broadcasted_iota(jnp.int32, (step, 2 * n), 0)
 
     def body(_, a):
@@ -72,20 +74,14 @@
             unit = (lane[:step] == row + at).astype(f32)
             col_r = [jnp.broadcast_to(a[:, at + m : at + m + 1], shape) for m in range(step)]
             col_i = [jnp.broadcast_to(a[:, n + at + m : n + at + m + 1], shape) for m in range(step)]
-            inv_r, inv_i = small_inverse(
-                [c[at : at + step] for c in col_r], [c[at : at + step] for c in col_i]
-            )
             top = jnp.where(swept[:step], unit, a[at : at + step])
             turned = swap(top, n) * sign
-            r = jnp.zeros_like(top)
-            ri = jnp.zeros_like(top)
-            for m in range(step):
-                tm, um = top[m : m + 1], turned[m : m + 1]
-                r = r + inv_r[m] * tm + inv_i[m] * um
-                ri = ri + inv_r[m] * um - inv_i[m] * tm
+            r, ri = sweep_rows(
+                [c[at : at + step] for c in col_r], [c[at : at + step] for c in col_i], top, turned
+            )
             rest = jnp.where(swept, 0.0, a)
             for m in range(step):
-                rest = rest - col_r[m] * r[m : m + 1] - col_i[m] * ri[m : m + 1]
+                rest = rest - col_r[m] * r[m : m + 1] + col_i[m] * ri[m : m + 1]
             pieces = [rest[:at], r, rest[at + step :]] if at else [r, rest[step:]]
             a = jnp.concatenate(pieces, axis=0)
         move = step * steps
@@ -109,9 +105,9 @@
 
 def kernel(
     poles, doms, y_hbm, ysep_hbm, green_hbm, pole_ref, coup_hbm, sep_hbm, rows_hbm,
-    out_ref, outsep_ref,
+    got, got_sep,
     ysep_ref, green_ref, coup_ref, sep_ref, rows_ref,
-    ybuf, part, part_sep, got, got_sep, sbuf, sgot, ebuf, egot, tbufs, tgots, xsends, xgots, first, maps,
+    ybuf, part, part_sep, sbuf, sgot, ebuf, egot, tbufs, tgots, xsends, xgots, first, maps,
     load, y_s, y_r, s_s, s_r, t_s, t_r, x_s, x_r, o_s, o_r, p_s, p_r,
 ):
     levels = doms.bit_length() - 1
@@ -148,15 +144,11 @@
         pl.semaphore_signal(barrier, inc=1, device_id=(peer, dom), device_id_type=MESH)
     for mate in mates:
         pl.semaphore_signal(barrier, inc=1, device_id=(pole, mate), device_id_type=MESH)
-    pl.semaphore_wait(barrier, len(peers) + len(mates))
-    y_copies = [
-        send(y_hbm, ybuf.at[pole], y_s.at[o], y_r.at[o], (peer, dom)) for o, peer in enumerate(peers)
-    ]
 
     s = sep_ref.shape[0]
     ni = green_ref.shape[1]
     m = y_hbm.shape[1]
-    zr, zi, wr, wi = pole_ref[0, 0], pole_ref[1, 0], pole_ref[2, 0], pole_ref[3, 0]
+    zr, zi, wr, wi = pole_ref[0], pole_ref[1], pole_ref[2], pole_ref[3]
     for copy in loads[:2]:
         copy.wait()
     spot = lax.broadcasted_iota(jnp.int32, (ni, rows_ref.shape[1]), 0)
@@ -171,6 +163,10 @@
     n_r = dot(c, green_ref[0])
     n_i = dot(c, green_ref[1])
     n_rs, n_is = split(n_r), split(n_i)
+    pl.semaphore_wait(barrier, len(peers) + len(mates))
+    y_copies = [
+        send(y_hbm, ybuf.at[pole], y_s.at[o], y_r.at[o], (peer, dom)) for o, peer in enumerate(peers)
+    ]
     k_r = dot(n_rs, c, 1, 1)
     k_i = dot(n_is, c, 1, 1)
     eye = (
@@ -353,7 +349,7 @@
 
     rows = ni // poles
     rows_sep = s // poles
-    o_copies, p_copies = [], []
+    o_copies, p_copies, own_copies = [], [], []
     for turn in range(halves):
         half = bits[0] if turn == 0 else 1 - bits[0]
         columns = pl.ds(pl.multiple_of(half * wide, wide), wide)
@@ -364,7 +360,9 @@
         for o, peer in enumerate(peers + [pole]):
             at = pl.ds(pl.multiple_of(peer * rows, rows), rows)
             part[turn, peer] = first[at, columns] + dot(maps[at, :], xhs, 1, 1)
-            if o < len(peers):
+            if o == len(peers):
+                own_copies.append(fetch(part.at[turn, peer], got.at[o, :, columns], 6 + turn))
+            else:
                 o_copies.append(
                     send(
                         part.at[turn, peer], got.at[o, :, columns],
@@ -378,21 +376,11 @@
         p_copies.append(
             send(part_sep.at[peer], got_sep.at[o], p_s.at[o], p_r.at[o], (peer, dom))
         )
-    for turn in range(halves):
-        half = bits[0] if turn == 0 else 1 - bits[0]
-        columns = pl.ds(pl.multiple_of(half * wide, wide), wide)
-        out_ref[:, columns] = part[turn, pole]
-    for copy in o_copies:
+    own_copies.append(fetch(part_sep.at[pole], got_sep.at[len(peers)], 8))
+    for copy in o_copies + p_copies:
         copy.wait_recv()
-    total = out_ref[...]
-    for o in range(len(peers)):
-        total = total + got[o]
-    out_ref[...] = total
-    total = part_sep[pole]
-    for o in range(len(peers)):
-        p_copies[o].wait_recv()
-        total = total + got_sep[o]
-    outsep_ref[...] = total
+    for copy in own_copies:
+        copy.wait()
     for copy in y_copies + s_copies + t_copies + x_copies + o_copies + p_copies:
         copy.wait_send()
 
@@ -404,7 +392,6 @@
     levels = doms.bit_length() - 1
     others = max(poles - 1, 1)
     b = iface_rows.shape[-1]
-    vmem = pl.BlockSpec(memory_space=pltpu.VMEM)
     hbm = pl.BlockSpec(memory_space=pl.ANY)
     dma = pltpu.SemaphoreType.DMA
     buf = lambda *shape: pltpu.VMEM(shape, f32)
@@ -414,11 +401,11 @@
     out, out_sep = pl.pallas_call(
         functools.partial(kernel, poles, doms),
         out_shape=(
-            jax.ShapeDtypeStruct((rows, m), f32),
-            jax.ShapeDtypeStruct((s // poles, m), f32),
+            jax.ShapeDtypeStruct((poles, rows, m), f32),
+            jax.ShapeDtypeStruct((poles, s // poles, m), f32),
         ),
         in_specs=[hbm, hbm, hbm, pl.BlockSpec(memory_space=pltpu.SMEM), hbm, hbm, hbm],
-        out_specs=(vmem, vmem),
+        out_specs=(hbm, hbm),
         scratch_shapes=[
             buf(s, m),
             buf(2, ni, ni),
@@ -428,8 +415,6 @@
             buf(poles, rows, m),
             buf(2, poles, rows, m // 2),
             buf(poles, s // poles, m),
-            buf(others, rows, m),
-            buf(others, s // poles, m),
             buf(max(levels - 1, 1), 2 * s, 4 * s),
             buf(max(levels - 1, 1), 2 * s, 4 * s),
             buf(s, 2 * s),
@@ -440,7 +425,7 @@
             [buf(2, w, c) for w, c in sizes] + [buf(2, m // 2, 4 * s)],
             buf(ni, m),
             buf(ni, 4 * s),
-            dma((6,)),
+            dma((9,)),
             dma((others,)), dma((others,)),
             dma((levels,)), dma((levels,)),
             dma((levels,)), dma((levels,)),
@@ -452,10 +437,10 @@
             collective_id=0, has_side_effects=True, vmem_limit_bytes=56 * 1024 * 1024
         ),
     )(
-        y_interior[0], y_separator[0], green[:, 0, 0], pole_data, coupling[0], sep_block[0],
+        y_interior[0], y_separator[0], green[:, 0, 0], pole_data[:, 0], coupling[0], sep_block[0],
         iface_rows[0],
     )
-    return out[None], out_sep[None]
+    return jnp.sum(out, axis=0)[None], jnp.sum(out_sep, axis=0)[None]
 
 
 def solution(mesh):

time: 52.1 us -> 49.6 us (0.952)
  local copies, waits for them, and re-layouts: 4.2 us -> 0 us
  other arithmetic: 0 us -> 3.19 us
  Pallas kernels: 46.9 us -> 45.5 us
    unnamed x3 -> x0, local copies, waits for them, and re-layouts: 4.2 us -> none
    reduce_sum x0 -> x2, other arithmetic: none -> 3.19 us  [shards(): return (jnp.sum(out, axis=0)[None], jnp.sum(out_sep, axis=0)[None])]
    pallas_call x1, Pallas kernels: 46.9 us -> 45.5 us  [shards(): pl.pallas_call(functools.partial(kernel, poles, doms), out_shape=(jax.Sha...]
where the time goes in v2:
time: 49.6 us; the launch traced here: 49.3 us
  Pallas kernels  45.5 us (92%)
  other arithmetic  3.19 us (6%)
  between operations  0.64 us (1%)
    pallas_call x1, Pallas kernels, shards(): pl.pallas_call(functools.partial(kernel, poles, doms), out_shape=(jax.Sha...  45.5 us
    reduce_sum x2, other arithmetic, shards(): return (jnp.sum(out, axis=0)[None], jnp.sum(out_sep, axis=0)[None])  3.19 us

profile of v2, /device:TPU:0, one launch (start us, length us, event | category | flops | bytes accessed | tf_op | source)
XLA Modules:
  0.0 49.3 jit_solution(13857922149625188150)
XLA Ops:
  0.6 45.5 %shard_map.86 = (f32[4,128,256]{2,1,0:T(8,128)}, f32[4,16,256]{2,1,0:T(8,128)}) custom-call(f32[128,256]{1,0:T(8,128)} %bitcast.10, f32[64,256]{1,0:T(8,128)} %bitcast.12, f32[2,512,512]{2,1,0:T(8,128)} %bitcast.9, f32[4]{0:T(128)} %bitcast.17, f32[2,64,128]{2,1,0:T(8,128)} %bitcast.13, f32[64,64]{1,0:T(8,128)} %bitcast.14, s32[2,128]{1,0:T(2,128)} %bitcast.16), custom_call_target="tpu_custom_call" | custom-call | tf_op jit(solution)/shard_map/pallas_call | solution.py:401
  46.2 1.7 %reduce_sum.18 = f32[128,256]{1,0:T(8,128)} reduce(f32[4,128,256]{2,1,0:T(8,128)} %get-tuple-element.4, f32[]{:T(128)} %constant.0.clone.1), dimensions={0}, to_apply=%region_0.0 | reduce | flops 98304 | bytes 655364 | tf_op jit(solution)/shard_map/reduce_sum | solution.py:443
  47.9 1.5 %reduce_sum.19 = f32[16,256]{1,0:T(8,128)} reduce(f32[4,16,256]{2,1,0:T(8,128)} %get-tuple-element.5, f32[]{:T(128)} %constant.0.clone.1), dimensions={0}, to_apply=%region_1.0 | reduce | flops 12288 | bytes 81924 | tf_op jit(solution)/shard_map/reduce_sum | solution.py:443

commit v3 on v2

--- a/solution.py
+++ b/solution.py
@@ -383,6 +383,11 @@
         copy.wait()
     for copy in y_copies + s_copies + t_copies + x_copies + o_copies + p_copies:
         copy.wait_send()
+
+
+def add_poles(got, got_sep, out_ref, outsep_ref):
+    out_ref[...] = jnp.sum(got[...], axis=0)
+    outsep_ref[...] = jnp.sum(got_sep[...], axis=0)
 
 
 def shards(poles, doms, y_interior, y_separator, green, pole_data, coupling, sep_block, iface_rows):
@@ -440,7 +445,18 @@
         y_interior[0], y_separator[0], green[:, 0, 0], pole_data[:, 0], coupling[0], sep_block[0],
         iface_rows[0],
     )
-    return jnp.sum(out, axis=0)[None], jnp.sum(out_sep, axis=0)[None]
+    vmem = pl.BlockSpec(memory_space=pltpu.VMEM)
+    out, out_sep = pl.pallas_call(
+        add_poles,
+        out_shape=(
+            jax.ShapeDtypeStruct((rows, m), f32),
+            jax.ShapeDtypeStruct((s // poles, m), f32),
+        ),
+        in_specs=[vmem, vmem],
+        out_specs=(vmem, vmem),
+        compiler_params=pltpu.CompilerParams(vmem_limit_bytes=56 * 1024 * 1024),
+    )(out, out_sep)
+    return out[None], out_sep[None]
 
 
 def solution(mesh):

time: 49.6 us -> 48.1 us (0.970)
  other arithmetic: 3.19 us -> 0 us
  Pallas kernels: 45.5 us -> 47.2 us
    reduce_sum x2 -> x0, other arithmetic: 3.19 us -> none  [shards(): return (jnp.sum(out, axis=0)[None], jnp.sum(out_sep, axis=0)[None])]
    pallas_call x0 -> x1, Pallas kernels: none -> 1.73 us  [shards(): pl.pallas_call(add_poles, out_shape=(jax.ShapeDtypeStruct((rows, m), f32)...]
where the time goes in v3:
time: 48.1 us; the launch traced here: 47.9 us
  Pallas kernels  47.2 us (98%)
  between operations  0.64 us (1%)
    pallas_call x1, Pallas kernels, shards(): pl.pallas_call(functools.partial(kernel, poles, doms), out_shape=(jax.Sha...  45.5 us
    pallas_call x1, Pallas kernels, shards(): pl.pallas_call(add_poles, out_shape=(jax.ShapeDtypeStruct((rows, m), f32)...  1.73 us

profile of v3, /device:TPU:0, one launch (start us, length us, event | category | flops | bytes accessed | tf_op | source)
XLA Modules:
  0.0 47.9 jit_solution(18345591179057039845)
XLA Ops:
  0.6 45.5 %shard_map.86 = (f32[4,128,256]{2,1,0:T(8,128)}, f32[4,16,256]{2,1,0:T(8,128)}) custom-call(f32[128,256]{1,0:T(8,128)} %bitcast.10, f32[64,256]{1,0:T(8,128)} %bitcast.11, f32[2,512,512]{2,1,0:T(8,128)} %bitcast.9, f32[4]{0:T(128)} %bitcast.15, f32[2,64,128]{2,1,0:T(8,128)} %bitcast.12, f32[64,64]{1,0:T(8,128)} %bitcast.13, s32[2,128]{1,0:T(2,128)} %bitcast.14), custom_call_target="tpu_custom_call" | custom-call | tf_op jit(solution)/shard_map/pallas_call | solution.py:406
  46.2 1.7 %shard_map.87 = (f32[128,256]{1,0:T(8,128)}, f32[16,256]{1,0:T(8,128)}) custom-call(f32[4,128,256]{2,1,0:T(8,128)} %get-tuple-element.6.got, f32[4,16,256]{2,1,0:T(8,128)} %get-tuple-element.7.got_sep), custom_call_target="tpu_custom_call" | custom-call | tf_op jit(solution)/shard_map/pallas_call | solution.py:449

commit v4 on v3

--- a/solution.py
+++ b/solution.py
@@ -116,7 +116,12 @@
     dom = lax.axis_index("dom")
     bits = [lax.rem(lax.div(dom, 1 << l), 2) for l in range(levels)]
     mates = [dom + (1 - 2 * bits[l]) * (1 << l) for l in range(levels)]
-    peers = [lax.rem(pole + o, poles) for o in range(1, poles)]
+    pole_bits = [lax.rem(lax.div(pole, 1 << b), 2) for b in range(poles.bit_length() - 1)]
+    flips = sorted(range(1, poles), key=lambda o: (-bin(o).count("1"), o))
+    peers = [
+        pole + sum((1 - 2 * bit) * (1 << b) for b, bit in enumerate(pole_bits) if o >> b & 1)
+        for o in flips
+    ]
 
     def fetch(src, dst, number):
         copy = pltpu.make_async_copy(src, dst, load.at[number])

time: 48.1 us -> 48 us (level)
  no operation moved by 1% of the time
where the time goes in v4:
time: 48 us; the launch traced here: 47.8 us
  Pallas kernels  47.2 us (98%)
  between operations  0.64 us (1%)
    pallas_call x1, Pallas kernels, shards(): pl.pallas_call(functools.partial(kernel, poles, doms), out_shape=(jax.Sha...  45.5 us
    pallas_call x1, Pallas kernels, shards(): pl.pallas_call(add_poles, out_shape=(jax.ShapeDtypeStruct((rows, m), f32)...  1.73 us

profile of v4, /device:TPU:0, one launch (start us, length us, event | category | flops | bytes accessed | tf_op | source)
XLA Modules:
  0.0 47.8 jit_solution(5757675791465761802)
XLA Ops:
  0.6 45.5 %shard_map.86 = (f32[4,128,256]{2,1,0:T(8,128)}, f32[4,16,256]{2,1,0:T(8,128)}) custom-call(f32[128,256]{1,0:T(8,128)} %bitcast.10, f32[64,256]{1,0:T(8,128)} %bitcast.11, f32[2,512,512]{2,1,0:T(8,128)} %bitcast.9, f32[4]{0:T(128)} %bitcast.15, f32[2,64,128]{2,1,0:T(8,128)} %bitcast.12, f32[64,64]{1,0:T(8,128)} %bitcast.13, s32[2,128]{1,0:T(2,128)} %bitcast.14), custom_call_target="tpu_custom_call" | custom-call | tf_op jit(solution)/shard_map/pallas_call | solution.py:411
  46.1 1.7 %shard_map.87 = (f32[128,256]{1,0:T(8,128)}, f32[16,256]{1,0:T(8,128)}) custom-call(f32[4,128,256]{2,1,0:T(8,128)} %get-tuple-element.6.got, f32[4,16,256]{2,1,0:T(8,128)} %get-tuple-element.7.got_sep), custom_call_target="tpu_custom_call" | custom-call | tf_op jit(solution)/shard_map/pallas_call | solution.py:454
